TPU v7x, 256 devices: a whole 4x4x8 slice. The times are simulated.
256 devices in a mesh: island: 32 (over x_hi, z, core), zero: 8 (over y, x_lo).
Axes of the slice: x: 4 (x_hi: 2, x_lo: 2; x = x_hi * 2 + x_lo), y: 4, z: 8, core: 2. Of those that a mesh axis runs over, the one named last changes fastest.
Arguments:
- params: float32 [32, 2048, 2048], P('island', 'zero'), may hold values from -6 to 6
- moment: bfloat16 [32, 2048, 2048], P('island', 'zero'), may hold values from -4 to 4
- second: bfloat16 [32, 2048, 2048], P('island', 'zero'), may hold values from 0.5 to 4
- active: bfloat16 [32, 4096, 2048], P('island', 'zero'), may hold values from -6 to 6
- target: bfloat16 [32, 4096, 2048], P('island', 'zero'), may hold values from -6 to 6
- row_ids: int32 [2, 32, 2048], P(None, 'island', 'zero'), may hold values from 0 to 511
- step_index: int32 [1], replicated, may hold values from 0 to 999
Outputs:
- params_out: float32 [32, 2048, 2048], P('island', 'zero')
- moment_out: bfloat16 [32, 2048, 2048], P('island', 'zero')
- second_out: bfloat16 [32, 2048, 2048], P('island', 'zero')
All inputs are finite; a program needn't handle non-finite values.
Results may differ from a plain program's by a relative error of at most 0.02.
Values may be sent and summed in bfloat16 or wider, within the bound.
A program may use at most 128 MiB of HBM per device.

v0:
```python
import math

import jax
import jax.numpy as jnp
from jax import lax
from jax.sharding import PartitionSpec as P

D = 2048
ITERS = 2


beta_mean = 0.9
beta_square = 0.95
step_rate = 0.02
epsilon_add = 1e-08
gossip_rate = 0.4


def for_sending(x):

    def short(part):
        return part.astype(jnp.bfloat16) if part.dtype == jnp.float32 else part

    return jax.tree.map(short, x)


def partner(x, axis, apart):
    return lax.ppermute(x, axis, [(i, i ^ 1 << apart) for i in range(lax.axis_size(axis))])


def cosine_table():
    places = jnp.arange(128, dtype=jnp.float32)[:, None]
    orders = jnp.arange(64, dtype=jnp.float32)[None, :]
    cosines = jnp.cos(math.pi * (places + 0.5) * orders / 128.0) * math.sqrt(2.0 / 128.0)
    return jnp.where(orders == 0.0, cosines * math.sqrt(0.5), cosines)


def compress(values, cosines):
    blocks = values.reshape(values.shape[:-1] + (-1, 128))
    coeffs = jnp.einsum("...bi,ik->...bk", blocks, cosines, precision=lax.Precision.HIGHEST)
    return coeffs.reshape(values.shape[:-1] + (-1,))


def expand(coeffs, cosines):
    blocks = coeffs.reshape(coeffs.shape[:-1] + (-1, 64))
    values = jnp.einsum("...bk,ik->...bi", blocks, cosines, precision=lax.Precision.HIGHEST)
    return values.reshape(coeffs.shape[:-1] + (-1,))


def partner_swap(degree):

    def swapped(packed):
        return jax.tree.map(
            lambda part, own: part.astype(own.dtype),
            partner(for_sending(packed), "island", degree),
            packed,
        )

    return swapped


def shards(params, moment, second, active, target, row_ids, step_index):
    cosines = cosine_table()
    levels = lax.axis_size("island").bit_length() - 1
    branches = [partner_swap(degree) for degree in range(levels)]
    master = params[0]
    mean_state = moment[0]
    square_state = second[0]
    out_width = master.shape[1]
    tokens = row_ids.shape[2]
    factor = 1.0 / math.sqrt(D * tokens * lax.axis_size("zero"))
    leftover = jnp.zeros(master.shape, jnp.float32)
    for iteration in range(ITERS):
        weights = master.astype(jnp.bfloat16)
        chosen = row_ids[iteration, 0]
        inputs = jnp.take(active[0], chosen, axis=0)
        wanted = jnp.take(target[0], chosen, axis=0)
        slab_rows = lax.all_gather(weights, "zero", axis=0, tiled=True)
        columns = lax.slice_in_dim(inputs, 0, slab_rows.shape[0], axis=1)
        output = jnp.zeros((tokens, out_width), jnp.float32) + jnp.dot(
            columns, slab_rows, preferred_element_type=jnp.float32
        )
        residual = (output - wanted.astype(jnp.float32)).astype(jnp.bfloat16)
        summed = lax.psum_scatter(
            jnp.dot(inputs.T, residual, preferred_element_type=jnp.float32).astype(jnp.bfloat16),
            "zero",
            scatter_dimension=0,
            tiled=True,
        ).astype(jnp.float32)
        grad = summed * factor
        mean_next = beta_mean * mean_state.astype(jnp.float32) + (1.0 - beta_mean) * grad
        square_next = (
            beta_square * square_state.astype(jnp.float32) + (1.0 - beta_square) * grad * grad
        )
        updated = master - step_rate * mean_next / (jnp.sqrt(square_next) + epsilon_add)
        mean_state = mean_next.astype(jnp.bfloat16)
        square_state = square_next.astype(jnp.bfloat16)
        carried = updated + leftover
        coeffs = compress(carried, cosines).astype(jnp.bfloat16)
        leftover = carried - expand(coeffs.astype(jnp.float32), cosines)
        degree_now = jnp.remainder(step_index[0] + iteration, levels)
        remote = lax.switch(degree_now, branches, coeffs)
        master = updated + gossip_rate * expand(
            remote.astype(jnp.float32) - coeffs.astype(jnp.float32), cosines
        )
    return (master[None], mean_state[None], square_state[None])


def solution(mesh):
    in_specs = (
        P("island", "zero", None),
        P("island", "zero", None),
        P("island", "zero", None),
        P("island", "zero", None),
        P("island", "zero", None),
        P(None, "island", "zero"),
        P(),
    )
    out_specs = (P("island", "zero", None), P("island", "zero", None), P("island", "zero", None))
    return jax.shard_map(shards, mesh=mesh, in_specs=in_specs, out_specs=out_specs, check_vma=False)
```

profile of v0, /device:TPU:6, one launch (start us, length us, event | category | flops | bytes accessed | tf_op | source)
XLA Modules:
  0.0 805.3 jit_solution(4306059607409636244)
XLA Ops:
  7.2 0.0 copy-start
  7.2 0.0 copy-start.7
  7.2 0.0 all-gather.3.cloned.1.call-start
  7.2 2.9 bitcast_convert_fusion
  10.1 0.0 all-gather.3.cloned.1.call-update
  10.1 0.0 reduce-scatter.3.cloned.1.call-start
  10.2 1.4 gather_fusion
  11.6 5.2 gather_fusion.1
  16.8 167.7 %all-gather.3.cloned.1.call-done = bf16[2048,2048]{1,0:T(8,128)(2,1)} async-done(((bf16[256,2048]{1,0:T(8,128)(2,1)}), bf16[2048,2048]{1,0:T(8,128)(2,1)}) %all-gather.3.cloned.1.call-update) | async-done | bytes 8388624 | tf_op jit(solution)/shard_map/all_gather | solution.py:78
  184.5 9.3 %convolution_convert_fusion.1 = bf16[2048,2048]{1,0:T(8,128)(2,1)} fusion(bf16[256,2048]{1,0:T(8,128)(2,1)S(1)} %gather_fusion, pred[256]{0:T(512)(128)(4,1)S(1)} %compare_and_fusion.1, bf16[2048,2048]{1,0:T(8,128)(2,1)} %all-gather.3.cloned.1.call-done, bf16[256,2048]{1,0:T(8,128)(2,1)} %gather_fusion.1), kind=kOutput, calls=%fused_computation.5 | convolution fusion | flops 4302307328 | bytes 18874624 | tf_op jit(solution)/shard_map/dot_general | solution.py:85
  193.8 0.0 reduce-scatter.3.cloned.1.call-update
  193.8 0.0 all-gather.5.cloned.1.call-start
  194.6 172.0 %reduce-scatter.3.cloned.1.call-done = bf16[256,2048]{1,0:T(8,128)(2,1)} async-done(((bf16[2048,2048]{1,0:T(8,128)(2,1)}), bf16[256,2048]{1,0:T(8,128)(2,1)}) %reduce-scatter.3.cloned.1.call-update) | async-done | bytes 1048592 | tf_op jit(solution)/shard_map/reduce_scatter | solution.py:84
  366.7 3.7 bitcast_subtract_fusion.1
  370.4 0.0 copy-start.2
  370.4 1.3 copy-done.2
  371.7 2.5 fusion.20
  374.3 0.2 copy.30
  374.5 14.0 %conditional.8 = (bf16[256,1024]{1,0:T(8,128)(2,1)}) conditional(s32[]{:T(128)} %clamp.6, bf16[256,1024]{1,0:T(8,128)(2,1)S(1)} %copy.30, bf16[256,1024]{1,0:T(8,128)(2,1)S(1)} %copy.30, bf16[256,1024]{1,0:T(8,128)(2,1)S(1)} %copy.30, bf16[256,1024]{1,0:T(8,128)(2,1)S(1)} %copy.30, ...), branch_computations={%region_1.3_spmd, %region_2.4_spmd, %region_3.5_spmd, %region_4.6_... | conditional | bytes 2097200
  374.5 1.6 collective-permute-start.1
  376.1 12.3 %collective-permute-done.1 = bf16[256,1024]{1,0:T(8,128)(2,1)} collective-permute-done((bf16[256,1024]{1,0:T(8,128)(2,1)S(1)}, bf16[256,1024]{1,0:T(8,128)(2,1)}, u32[]{:S(2)}, u32[]{:S(2)}) %collective-permute-start.1) | collective-permute-done | bytes 524320 | tf_op jit(solution)/shard_map/cond/branch_1_fun/ppermute | solution.py:28
  388.4 1.2 copy.35
  389.7 0.1 convert_subtract_fusion.1
  389.8 3.3 convolution_multiply_fusion.1
  393.2 2.9 copy.48
  396.1 4.3 fusion.78
  400.4 0.0 all-gather.5.cloned.1.call-update
  400.4 0.3 reduce-scatter.5.cloned.1.call-start
  400.7 2.3 gather_fusion.2
  403.0 4.3 gather_fusion.3
  407.4 165.1 %all-gather.5.cloned.1.call-done = bf16[2048,2048]{1,0:T(8,128)(2,1)} async-done(((bf16[256,2048]{1,0:T(8,128)(2,1)}), bf16[2048,2048]{1,0:T(8,128)(2,1)}) %all-gather.5.cloned.1.call-update) | async-done | bytes 8388624 | tf_op jit(solution)/shard_map/all_gather | solution.py:78
  572.5 9.1 %convolution_convert_fusion = bf16[2048,2048]{1,0:T(8,128)(2,1)} fusion(bf16[256,2048]{1,0:T(8,128)(2,1)S(1)} %copy-done.6, pred[256]{0:T(512)(128)(4,1)S(1)} %compare_and_fusion, bf16[2048,2048]{1,0:T(8,128)(2,1)} %all-gather.5.cloned.1.call-done, bf16[256,2048]{1,0:T(8,128)(2,1)S(1)} %gather_fusion.3), kind=kOutput, calls=%fused_computation.4 | convolution fusion | flops 4302307328 | bytes 18874624 | tf_op jit(solution)/shard_map/dot_general | solution.py:85
  581.6 0.0 reduce-scatter.5.cloned.1.call-update
  581.7 0.0 copy-start.3
  581.7 1.9 copy.46
  583.5 3.8 fusion.30
  587.3 167.2 %reduce-scatter.5.cloned.1.call-done = bf16[256,2048]{1,0:T(8,128)(2,1)} async-done(((bf16[2048,2048]{1,0:T(8,128)(2,1)}), bf16[256,2048]{1,0:T(8,128)(2,1)}) %reduce-scatter.5.cloned.1.call-update) | async-done | bytes 1048592 | tf_op jit(solution)/shard_map/reduce_scatter | solution.py:84
  754.5 5.9 fusion.9
  760.4 2.5 fusion.23
  763.0 0.2 copy.39
  763.2 26.3 %conditional.9 = (bf16[256,1024]{1,0:T(8,128)(2,1)}) conditional(s32[]{:T(128)} %clamp.7, bf16[256,1024]{1,0:T(8,128)(2,1)S(1)} %copy.39, bf16[256,1024]{1,0:T(8,128)(2,1)S(1)} %copy.39, bf16[256,1024]{1,0:T(8,128)(2,1)S(1)} %copy.39, bf16[256,1024]{1,0:T(8,128)(2,1)S(1)} %copy.39, ...), branch_computations={%region_7.9_spmd, %region_8.10_spmd, %region_9.11_spmd, %region_10... | conditional | bytes 2097200
  763.5 2.6 collective-permute-start.7
  766.1 23.4 %collective-permute-done.7 = bf16[256,1024]{1,0:T(8,128)(2,1)} collective-permute-done((bf16[256,1024]{1,0:T(8,128)(2,1)S(1)}, bf16[256,1024]{1,0:T(8,128)(2,1)}, u32[]{:S(2)}, u32[]{:S(2)}) %collective-permute-start.7) | collective-permute-done | bytes 524320 | tf_op jit(solution)/shard_map/cond/branch_2_fun/ppermute | solution.py:28
  789.5 1.2 copy.44
  790.7 0.1 convert_subtract_fusion
  790.9 2.0 convolution_multiply_fusion
  792.9 1.8 copy.49
  794.7 4.0 add_bitcast_fusion
  (20 shorter events, 0.1 us)
Async XLA Ops:
  7.2 3.0 copy-start
  7.2 3.0 copy-start.7
  7.2 177.3 %all-gather.3.cloned.1.call-start = ((), (), s32[]{:S(2)}) async-start(), calls=%async_computation.2 | async-start | bytes 9437184 | tf_op jit(solution)/shard_map/all_gather | solution.py:78
  10.1 356.5 %reduce-scatter.3.cloned.1.call-start = ((), (), s32[]{:S(2)}) async-start(), calls=%async_computation.3 | async-start | bytes 9437184 | tf_op jit(solution)/shard_map/reduce_scatter | solution.py:84
  193.8 172.9 %copy-start.4 = (bf16[1,256,2048]{2,1,0:T(8,128)(2,1)S(1)}, bf16[1,256,2048]{2,1,0:T(8,128)(2,1)}, u32[]{:S(2)}) copy-start(bf16[1,256,2048]{2,1,0:T(8,128)(2,1)} %param.20) | copy-start | bytes 3145732
  193.8 378.6 %all-gather.5.cloned.1.call-start = ((), (), s32[]{:S(2)}) async-start(), calls=%async_computation.4 | async-start | bytes 9437184 | tf_op jit(solution)/shard_map/all_gather | solution.py:78
  370.4 1.3 copy-start.2
  374.5 13.9 %collective-permute-start.1 = (bf16[256,1024]{1,0:T(8,128)(2,1)S(1)}, bf16[256,1024]{1,0:T(8,128)(2,1)}, u32[]{:S(2)}, u32[]{:S(2)}) collective-permute-start(bf16[256,1024]{1,0:T(8,128)(2,1)S(1)} %param.3), channel_id=1, source_target_pairs={{0,16},{8,24},{16,0},{24,8},{32,48},{40,56},{48,32},{56,40},{64,80... | collective-permute-start | bytes 1572872 | tf_op jit(solution)/shard_map/cond/branch_1_fun/ppermute | solution.py:28
  400.4 354.1 %reduce-scatter.5.cloned.1.call-start = ((), (), s32[]{:S(2)}) async-start(), calls=%async_computation.5 | async-start | bytes 9437184 | tf_op jit(solution)/shard_map/reduce_scatter | solution.py:84
  403.0 169.4 %copy-start.6 = (bf16[256,2048]{1,0:T(8,128)(2,1)S(1)}, bf16[256,2048]{1,0:T(8,128)(2,1)}, u32[]{:S(2)}) copy-start(bf16[256,2048]{1,0:T(8,128)(2,1)} %gather_fusion.2) | copy-start | bytes 3145732
  581.7 172.8 %copy-start.3 = (f32[256,2048]{1,0:T(8,128)S(1)}, f32[256,2048]{1,0:T(8,128)}, u32[]{:S(2)}) copy-start(f32[256,2048]{1,0:T(8,128)} %copy-done.2) | copy-start | bytes 6291460
  583.5 171.0 %copy-start.5 = (bf16[1,256,2048]{2,1,0:T(8,128)(2,1)S(1)}, bf16[1,256,2048]{2,1,0:T(8,128)(2,1)}, u32[]{:S(2)}) copy-start(bf16[1,256,2048]{2,1,0:T(8,128)(2,1)} %param.20) | copy-start | bytes 3145732
  763.5 26.0 %collective-permute-start.7 = (bf16[256,1024]{1,0:T(8,128)(2,1)S(1)}, bf16[256,1024]{1,0:T(8,128)(2,1)}, u32[]{:S(2)}, u32[]{:S(2)}) collective-permute-start(bf16[256,1024]{1,0:T(8,128)(2,1)S(1)} %param.9), channel_id=1, source_target_pairs={{0,32},{8,40},{16,48},{24,56},{32,0},{40,8},{48,16},{56,24},{64,96... | collective-permute-start | bytes 1572872 | tf_op jit(solution)/shard_map/cond/branch_2_fun/ppermute | solution.py:28
  794.7 4.0 copy-start.1
Sparse Core Ops, SparseCore 0:
  10.4 174.1 all-gather.2
  193.9 172.6 reduce-scatter.2
  400.5 171.8 all-gather.4
  581.8 172.6 reduce-scatter.4
where the time goes:
time: 806 us; the launch traced here: 805 us
  waiting for transfers between devices  708 us (88%)
  matrix products  32.6 us (4%)
  local copies, waits for them, and re-layouts  24 us (3%)
  other arithmetic  21.2 us (3%)
  between operations  14.7 us (2%)
    reduce_scatter x2, waiting for transfers between devices, shards(): lax.psum_scatter(jnp.dot(inputs.T, residual, preferred_element_type=jnp.f...  339 us
    all_gather x2, waiting for transfers between devices, shards(): slab_rows = lax.all_gather(weights, 'zero', axis=0, tiled=True)  333 us
    ppermute x2, waiting for transfers between devices, partner(): lax.ppermute(x, axis, [(i, i ^ 1 << apart) for i in range(lax.axis_size(a...  35.7 us
    dot_general x2, matrix products, shards(): jnp.dot(inputs.T, residual, preferred_element_type=jnp.float32)  18.4 us
  transfers between devices with their start and end apart: 6, of which 6 were waited for; matrix products, arithmetic and copies ran while one was open for 2% of the time, Pallas kernels for 0%

commit v1 on v0

v1 whole, which is shorter than its diff:
```python
import functools
import math

import jax
import jax.numpy as jnp
import numpy as np
from jax import lax
from jax.experimental import pallas as pl
from jax.experimental.pallas import tpu as pltpu
from jax.sharding import PartitionSpec as P

MESH = pl.DeviceIdType.MESH
BF16 = jnp.bfloat16
F32 = jnp.float32

ITERS = 2
NY = 4
NX = 2
S = 4

beta_mean = 0.9
beta_square = 0.95
step_rate = 0.02
epsilon_add = 1e-08
gossip_rate = 0.4


def cosine_tables():
    places = np.arange(128)[:, None]
    orders = np.arange(64)[None, :]
    one = np.cos(math.pi * (places + 0.5) * orders / 128.0) * math.sqrt(2.0 / 128.0)
    one = np.where(orders == 0, one * math.sqrt(0.5), one)
    two = np.zeros((256, 128))
    two[:128, :64] = one
    two[128:, 64:] = one
    two = two.astype(np.float32)
    high = two.astype(jnp.bfloat16)
    low = (two - high.astype(np.float32)).astype(jnp.bfloat16)
    return high, low, np.ascontiguousarray(high.T), np.ascontiguousarray(low.T)


def dot(a, b):
    return jnp.dot(a, b, preferred_element_type=F32)


def kernel(
    bits,
    params_in, moment_in, second_in, act, tgt, ids, ch, cl, eh, el,
    params_out, moment_out, second_out,
    master, mean, square, left, x_all, x_turn, y_send, y_all, w_send, w_all,
    res, own, gx_send, gx_recv, gy_send, gy_recv, c_send, c_recv,
    in_sem, out_sem,
    xa_s, xa_r, ya_s, ya_r, wy_s, wy_r, wx_s, wx_r, gx_s, gx_r, gy_s, gy_r, c_s, c_r,
):
    rows, width = master.shape
    tokens = ids.shape[1]
    stored = act.shape[0]
    depth = act.shape[1]
    chunk = width // S
    part = chunk // NY
    half = depth // NX
    island = lax.axis_index("island")
    z = lax.axis_index("zero")
    x = lax.rem(z, NX)
    y = lax.div(z, NX)
    other = 1 - x
    factor = 1.0 / math.sqrt(depth * tokens * NX * NY)

    def along_y(dy):
        return (island, lax.rem(y + dy, NY) * NX + x)

    across = (island, y * NX + other)
    partners = []
    for bit in bits:
        apart = 2**bit
        partners.append((island + apart * (1 - 2 * lax.rem(lax.div(island, apart), 2)), z))

    barrier = pltpu.get_barrier_semaphore()
    friends = [along_y(1), along_y(2), along_y(3), across] + partners
    for friend in friends:
        pl.semaphore_signal(barrier, inc=1, device_id=friend, device_id_type=MESH)

    started = []

    def send(src, dst, s_sem, r_sem, device):
        copy = pltpu.make_async_remote_copy(
            src_ref=src, dst_ref=dst, send_sem=s_sem, recv_sem=r_sem,
            device_id=device, device_id_type=MESH,
        )
        copy.start()
        started.append(copy)
        return copy

    loads = []
    for s in range(S):
        cols = pl.ds(s * chunk, chunk)
        loads.append(pltpu.make_async_copy(params_in.at[:, cols], master.at[:, cols], in_sem.at[s]))
    loads.append(pltpu.make_async_copy(moment_in, mean, in_sem.at[S]))
    loads.append(pltpu.make_async_copy(second_in, square, in_sem.at[S + 1]))
    for load in loads:
        load.start()

    def selector(k):
        spots = lax.broadcasted_iota(jnp.int32, (stored, tokens), 0)
        return jnp.where(spots == ids[k : k + 1, :], 1.0, 0.0).astype(F32).T.astype(BF16)

    def pick_x(k):
        pick = selector(k)
        for b in range(NX * NY):
            to = (b % NX) * NY + b // NX
            block = dot(pick, act[:, b * rows : (b + 1) * rows])
            x_all[k, 0:tokens, to * rows : (to + 1) * rows] = block.astype(BF16)

    def pick_y(k):
        pick = selector(k)
        for s in range(S):
            block = dot(pick, tgt[:, s * chunk : (s + 1) * chunk]).astype(BF16)
            for q in range(NY):
                y_send[k, s, q] = block[:, q * part : (q + 1) * part]

    def turn(k, slot):
        def step(b, _):
            at = pl.multiple_of(b * rows, rows)
            block = x_all[k, slot * tokens : (slot + 1) * tokens, pl.ds(at, rows)]
            x_turn[k, pl.ds(at, rows), slot * tokens : (slot + 1) * tokens] = block.T
            return 0

        lax.fori_loop(0, depth // rows, step, 0)

    upper = pl.ds(0, tokens // 2)
    lower = pl.ds(tokens // 2, tokens // 2)

    def x_rows(k, slot, which):
        return x_all.at[k, pl.ds(slot * tokens + which * (tokens // 2), tokens // 2)]

    xs = {}

    def x_first(k):
        for n, (which, dy, slot) in enumerate(((0, 1, 1), (1, 3, 2), (1, 1, 1), (0, 3, 2))):
            xs[k, n] = send(
                x_rows(k, 0, which), x_rows(k, slot, which), xa_s.at[k, n], xa_r.at[k, n], along_y(dy)
            )

    def x_second(k):
        xs[k, 0].wait_recv()
        xs[k, 4] = send(x_rows(k, 1, 0), x_rows(k, 3, 0), xa_s.at[k, 4], xa_r.at[k, 4], along_y(1))
        xs[k, 1].wait_recv()
        xs[k, 5] = send(x_rows(k, 2, 1), x_rows(k, 3, 1), xa_s.at[k, 5], xa_r.at[k, 5], along_y(3))

    def x_last(k):
        xs[k, 2].wait_recv()
        turn(k, 1)
        xs[k, 3].wait_recv()
        turn(k, 2)
        xs[k, 4].wait_recv()
        xs[k, 5].wait_recv()
        turn(k, 3)

    slot_of = {1: 1, 3: 2, 2: 3}
    ys, wys, wxs, gxs, gys, cs = {}, {}, {}, {}, {}, {}

    def y_first(k, s):
        for n, dy in enumerate((1, 3, 2)):
            ys[k, s, n] = send(
                y_send.at[k, s, lax.rem(y + dy, NY)], y_all.at[k, s, slot_of[dy]],
                ya_s.at[k, s, n], ya_r.at[k, s, n], along_y(dy),
            )
        y_all[k, s, 0] = y_send[k, s, y]

    def w_first(k, s):
        for q in range(NY):
            at = s * chunk + q * part
            w_send[k, s, q] = master[:, at : at + part].astype(BF16)
        mine = pl.ds(pl.multiple_of((x * NY + y) * rows, rows), rows)
        for n, dy in enumerate((1, 3, 2)):
            wys[k, s, n] = send(
                w_send.at[k, s, lax.rem(y + dy, NY)], w_all.at[k, s, mine],
                wy_s.at[k, s, n], wy_r.at[k, s, n], along_y(dy),
            )
        w_all[k, s, mine] = w_send[k, s, y]

    def w_second(k, s):
        for n in range(3):
            wys[k, s, n].wait_recv()
        mine = w_all.at[k, s, pl.ds(pl.multiple_of(x * half, half), half)]
        wxs[k, s] = send(mine, mine, wx_s.at[k, s], wx_r.at[k, s], across)

    def work(k, s):
        if s == 0:
            x_last(k)
        for n in range(3):
            ys[k, s, n].wait_recv()
        wxs[k, s].wait_recv()
        for slot in range(NY):
            at = slot * tokens
            out = dot(x_all[k, at : at + tokens, :], w_all[k, s])
            res[at : at + tokens, :] = (out - y_all[k, s, slot].astype(F32)).astype(BF16)

        def term(side, b):
            at = pl.multiple_of(side * half + b * rows, rows)
            return dot(x_turn[k, pl.ds(at, rows), :], res[...])

        for b in range(NY):
            gx_send[k, s, b] = term(other, b).astype(BF16)
        gxs[k, s] = send(gx_send.at[k, s], gx_recv.at[k, s], gx_s.at[k, s], gx_r.at[k, s], across)
        for b in range(NY):
            own[s, b] = term(x, b)

    def add(k, s):
        gxs[k, s].wait_recv()
        for b in range(NY):
            gy_send[k, s, b] = (own[s, b] + gx_recv[k, s, b].astype(F32)).astype(BF16)
        for n, dy in enumerate((1, 3, 2)):
            gys[k, s, n] = send(
                gy_send.at[k, s, lax.rem(y + dy, NY)], gy_recv.at[k, s, y],
                gy_s.at[k, s, n], gy_r.at[k, s, n], along_y(dy),
            )
        gy_recv[k, s, y] = gy_send[k, s, y]

    def expand(c):
        return dot(c, eh[...]) + dot(c, el[...])

    def update(k, s):
        for n in range(3):
            gys[k, s, n].wait_recv()
        if k == 0 and s == 0:
            loads[S].wait()
            loads[S + 1].wait()
        wide = 256
        for j in range(chunk // wide):
            at = s * chunk + j * wide
            cols = slice(at, at + wide)
            per = wide // part
            grad = jnp.concatenate([gy_recv[k, s, j * per + q] for q in range(per)], axis=1)
            grad = grad.astype(F32) * factor
            mean_next = beta_mean * mean[:, cols].astype(F32) + (1.0 - beta_mean) * grad
            square_next = beta_square * square[:, cols].astype(F32) + (1.0 - beta_square) * grad * grad
            mean[:, cols] = mean_next.astype(BF16)
            square[:, cols] = square_next.astype(BF16)
            updated = master[:, cols] - step_rate * mean_next / (jnp.sqrt(square_next) + epsilon_add)
            carried = updated if k == 0 else updated + left[:, cols]
            high = carried.astype(BF16)
            low = (carried - high.astype(F32)).astype(BF16)
            coeffs = (dot(high, ch[...]) + (dot(low, ch[...]) + dot(high, cl[...]))).astype(BF16)
            c_send[k, s, :, j * (wide // 2) : (j + 1) * (wide // 2)] = coeffs
            back = expand(coeffs)
            if k + 1 < ITERS:
                left[:, cols] = carried - back
            master[:, cols] = updated - gossip_rate * back
        cs[k, s] = send(c_send.at[k, s], c_recv.at[k, s], c_s.at[k, s], c_r.at[k, s], partners[k])
        if k + 1 == ITERS:
            put(mean, moment_out, s, 1)
            put(square, second_out, s, 2)

    stores = []

    def put(src, dst, s, n):
        cols = pl.ds(s * chunk, chunk)
        copy = pltpu.make_async_copy(src.at[:, cols], dst.at[:, cols], out_sem.at[n, s])
        copy.start()
        stores.append(copy)

    def gossip(k, s):
        cs[k, s].wait_recv()
        wide = 256
        for j in range(chunk // wide):
            at = s * chunk + j * wide
            remote = c_recv[k, s, :, j * (wide // 2) : (j + 1) * (wide // 2)]
            master[:, at : at + wide] = master[:, at : at + wide] + gossip_rate * expand(remote)
        if k + 1 == ITERS:
            put(master, params_out, s, 0)
        else:
            w_first(k + 1, s)

    pick_x(0)
    loads[0].wait()
    pl.semaphore_wait(barrier, len(friends))
    w_first(0, 0)
    x_first(0)
    pick_y(0)
    y_first(0, 0)
    turn(0, 0)
    w_second(0, 0)
    x_second(0)
    for s in range(1, S):
        loads[s].wait()
        w_first(0, s)
        y_first(0, s)
    pick_x(1)
    pick_y(1)
    turn(1, 0)

    stages = [w_second, work, add, update, gossip]
    line = [(stage, k) for k in range(ITERS) for stage in stages]
    for t in range(len(line) + S - 1):
        if t == 2:
            x_first(1)
        if t == 4:
            x_second(1)
            for s in range(S):
                y_first(1, s)
        for s in range(S):
            if 0 <= t - s < len(line):
                stage, k = line[t - s]
                if (stage, k, s) != (w_second, 0, 0):
                    stage(k, s)

    for copy in started:
        copy.wait_send()
    for copy in stores:
        copy.wait()


def window(bits, collective_id, params, moment, second, active, target, ids, tables):
    rows, width = params.shape
    depth = active.shape[1]
    tokens = ids.shape[1]
    chunk = width // S
    part = chunk // NY
    group = tokens * NY
    half = depth // NX
    vmem = pl.BlockSpec(memory_space=pltpu.VMEM)
    anywhere = pl.BlockSpec(memory_space=pl.ANY)
    k = ITERS
    dma = pltpu.SemaphoreType.DMA
    scratch = [
        pltpu.VMEM((rows, width), F32),
        pltpu.VMEM((rows, width), BF16),
        pltpu.VMEM((rows, width), BF16),
        pltpu.VMEM((rows, width), F32),
        pltpu.VMEM((k, group, depth), BF16),
        pltpu.VMEM((k, depth, group), BF16),
        pltpu.VMEM((k, S, NY, tokens, part), BF16),
        pltpu.VMEM((k, S, NY, tokens, part), BF16),
        pltpu.VMEM((k, S, NY, rows, part), BF16),
        pltpu.VMEM((k, S, depth, part), BF16),
        pltpu.VMEM((group, part), BF16),
        pltpu.VMEM((S, NY, rows, part), F32),
        pltpu.VMEM((k, S, NY, rows, part), BF16),
        pltpu.VMEM((k, S, NY, rows, part), BF16),
        pltpu.VMEM((k, S, NY, rows, part), BF16),
        pltpu.VMEM((k, S, NY, rows, part), BF16),
        pltpu.VMEM((k, S, rows, chunk // 2), BF16),
        pltpu.VMEM((k, S, rows, chunk // 2), BF16),
        dma((S + 2,)),
        dma((3, S)),
    ]
    for shape in ((k, 6), (k, S, 3), (k, S, 3), (k, S), (k, S), (k, S, 3), (k, S)):
        scratch += [dma(shape), dma(shape)]
    return pl.pallas_call(
        functools.partial(kernel, bits),
        out_shape=(
            jax.ShapeDtypeStruct(params.shape, F32),
            jax.ShapeDtypeStruct(moment.shape, BF16),
            jax.ShapeDtypeStruct(second.shape, BF16),
        ),
        in_specs=[anywhere] * 3 + [vmem] * 7,
        out_specs=(anywhere,) * 3,
        scratch_shapes=scratch,
        compiler_params=pltpu.CompilerParams(
            collective_id=collective_id, has_side_effects=True, vmem_limit_bytes=62 * 2**20
        ),
        cost_estimate=pl.CostEstimate(flops=2 * 10**10, bytes_accessed=2 * 10**7, transcendentals=0),
        name=f"window_{collective_id}",
    )(params, moment, second, active, target, ids, *tables)


def shards(params, moment, second, active, target, row_ids, step_index):
    levels = lax.axis_size("island").bit_length() - 1
    tables = [jnp.asarray(t) for t in cosine_tables()]
    branches = [
        functools.partial(window, tuple((b + k) % levels for k in range(ITERS)), b)
        for b in range(levels)
    ]
    out = lax.switch(
        jnp.remainder(step_index[0], levels),
        branches,
        params[0], moment[0], second[0], active[0], target[0], row_ids[:, 0, :], tables,
    )
    return tuple(o[None] for o in out)


def solution(mesh):
    in_specs = (
        P("island", "zero", None),
        P("island", "zero", None),
        P("island", "zero", None),
        P("island", "zero", None),
        P("island", "zero", None),
        P(None, "island", "zero"),
        P(),
    )
    out_specs = (P("island", "zero", None), P("island", "zero", None), P("island", "zero", None))
    return jax.shard_map(shards, mesh=mesh, in_specs=in_specs, out_specs=out_specs, check_vma=False)
```

time: 806 us -> 218 us (0.27)
  waiting for transfers between devices: 708 us -> 0 us
  Pallas kernels: 0 us -> 185 us
  matrix products: 32.6 us -> 0 us
  other arithmetic: 21.2 us -> 0 us
  loops' own time: 0.31 us -> 21.4 us
  local copies, waits for them, and re-layouts: 24 us -> 6.39 us
  between operations: 14.7 us -> 1.61 us
    reduce_scatter x2 -> x0, waiting for transfers between devices: 339 us -> none  [shards(): lax.psum_scatter(jnp.dot(inputs.T, residual, preferred_element_type=jnp.f...]
    all_gather x2 -> x0, waiting for transfers between devices: 333 us -> none  [shards(): slab_rows = lax.all_gather(weights, 'zero', axis=0, tiled=True)]
    pallas_call x0 -> x1, Pallas kernels: none -> 185 us  [window(): pl.pallas_call(functools.partial(kernel, bits), out_shape=(jax.ShapeDtype...]
    ppermute x2 -> x0, waiting for transfers between devices: 35.7 us -> none  [partner(): lax.ppermute(x, axis, [(i, i ^ 1 << apart) for i in range(lax.axis_size(a...]
    dot_general x7 -> x0, matrix products: 32.6 us -> none  [the longest x2 18.4 us: shards(): jnp.dot(inputs.T, residual, preferred_element_type=jnp.float32)]
    another operation x0 -> x1, loops' own time: none -> 21.4 us  [shards(): lax.switch(jnp.remainder(step_index[0], levels), branches, params[0], mom...]
    gather x4 -> x0, local copies, waits for them, and re-layouts: 13.2 us -> none  [the longest x2 9.51 us: shards(): wanted = jnp.take(target[0], chosen, axis=0)]
  transfers between devices with their start and end apart: 6 -> 0, of which waited for: 6 -> 0; matrix products, arithmetic and copies ran while one was open for 2% -> 0% of each run, Pallas kernels for 0% -> 0%
where the time goes in v1:
time: 218 us; the launch traced here: 215 us
  Pallas kernels  185 us (85%)
  loops' own time  21.4 us (10%)
  local copies, waits for them, and re-layouts  6.39 us (3%)
    pallas_call x1, Pallas kernels, window(): pl.pallas_call(functools.partial(kernel, bits), out_shape=(jax.ShapeDtype...  185 us
    another operation x1, loops' own time, shards(): lax.switch(jnp.remainder(step_index[0], levels), branches, params[0], mom...  21.4 us
    unnamed x6, local copies, waits for them, and re-layouts  6.39 us

profile of v1, /device:TPU:6, one launch (start us, length us, event | category | flops | bytes accessed | tf_op | source)
XLA Modules:
  0.0 214.8 jit_solution(3758510935181980497)
XLA Ops:
  1.3 0.7 copy.16
  2.0 206.8 %conditional.1 = ((f32[256,2048]{1,0:T(8,128)}, bf16[256,2048]{1,0:T(8,128)(2,1)S(1)}, bf16[256,2048]{1,0:T(8,128)(2,1)})) conditional(s32[]{:T(128)} %clamp.3, (f32[256,2048]{1,0:T(8,128)}, bf16[256,2048]{1,0:T(8,128)(2,1)}, bf16[256,2048]{1,0:T(8,128)(2,1)}, bf16[512,2048]{1,0:T(8,128)(2,1)}, ...), branch_computations={%region_0.1_spmd, %region_1.2_spmd, %region_2.3_spmd, %region_3.4_... | conditional | flops 20000000000 | bytes 20000008 | solution.py:375
  2.0 185.4 %window_0.1 = (f32[256,2048]{1,0:T(8,128)}, bf16[256,2048]{1,0:T(8,128)(2,1)S(1)}, bf16[256,2048]{1,0:T(8,128)(2,1)}) custom-call(f32[256,2048]{1,0:T(8,128)} %get-tuple-element.118.params_in, bf16[256,2048]{1,0:T(8,128)(2,1)} %get-tuple-element.119.moment_in, bf16[256,2048]{1,0:T(8,128)(2,1)} %get-tuple-element.120.second_in, ...), custom_call_target="tpu_custom_call" | custom-call | flops 20000000000 | bytes 20000000 | tf_op jit(solution)/shard_map/cond/branch_0_fun/window_0/pallas_call | solution.py:350
  208.8 3.1 %copy.36 = f32[1,256,2048]{2,1,0:T(8,128)} copy(f32[1,256,2048]{2,1,0:T(8,128)} %bitcast.12) | data formatting | bytes 4194304
  211.9 0.0 copy-start
  211.9 1.0 copy.37
  212.9 0.6 copy-done
  213.5 1.0 copy.38
Async XLA Ops:
  211.9 1.6 copy-start
